TPU v7x, 32 devices: a whole 2x2x4 slice. The times are simulated.
32 devices in a mesh: parts: 2 (over y), node: 4 (over x, core), local: 4 (over z).
Axes of the slice: x: 2, y: 2, z: 4, core: 2. Of those that a mesh axis runs over, the one named last changes fastest.
Arguments:
- tokens: bfloat16 [4096, 3584], P(('parts', 'node', 'local')), parts along dimension 0, may hold values from -6 to 6
- expert_ids: int32 [4096, 3], P(('parts', 'node', 'local')), parts along dimension 0, may hold values from 0 to 15, all different within a row; in each aligned block of 128 rows (0 to 127, 128 to 255, ...) at most 32 rows name the same one
- gate_weights: float32 [4096, 3], P(('parts', 'node', 'local')), parts along dimension 0, may hold values from 0.1 to 1
- gate_proj: bfloat16 [16, 3584, 1024], P(('node', 'local')), may hold values from -0.09375 to 0.09375
- up_proj: bfloat16 [16, 3584, 1024], P(('node', 'local')), may hold values from -0.09375 to 0.09375
- down_proj: bfloat16 [16, 1024, 3584], P(('node', 'local')), may hold values from -0.1875 to 0.1875
Outputs:
- combined: bfloat16 [4096, 3584], P(('parts', 'node', 'local')), parts along dimension 0
There are 2 independent parts, one for each index of `parts`. A program takes and returns all parts, laid end to end along the dimension named above; an argument that names none is the same for every part. Nothing has to cross between parts.
Inputs may be any that keep to these rules, and one draw needn't show every extreme that they name: `expert_ids`: each row names 3 different experts; among the rows of one device no expert is named by more than 32 rows, a bound that some block reaches.
All inputs are finite; a program needn't handle non-finite values.
Results may differ from a plain program's by a relative error of at most 0.0058.
Values may be sent and summed in bfloat16 or wider, within the bound.
A program may use at most 128 MiB of HBM per device.

v0:
```python
import jax
import jax.numpy as jnp
from jax import lax
from jax.sharding import PartitionSpec as P

EPG = 4


def expert_rows(received, gate_mat, up_mat, down_mat):
    features = received.shape[-1]
    flattened = received.reshape(-1, features)
    gate_act = jnp.dot(flattened, gate_mat, preferred_element_type=jnp.float32)
    up_act = jnp.dot(flattened, up_mat, preferred_element_type=jnp.float32)
    hidden = (jax.nn.silu(gate_act) * up_act).astype(jnp.bfloat16)
    output = jnp.dot(hidden, down_mat, preferred_element_type=jnp.float32).astype(jnp.bfloat16)
    return output.reshape(received.shape)


def on_device(tokens, expert_ids, gate_weights, gate_proj, up_proj, down_proj):
    tok_dev = tokens.shape[0]
    features = tokens.shape[1]
    top_count = expert_ids.shape[1]
    node_count = lax.axis_size("node")
    local_count = lax.axis_size("local")
    experts = EPG * node_count
    wsplit = local_count // EPG
    capacity = 4 * tok_dev * top_count // (3 * experts)
    matches = expert_ids[:, :, None] == jnp.arange(experts, dtype=jnp.int32)[None, None, :]
    chosen = jnp.sum(matches.astype(jnp.int32), axis=1)
    ranking = jnp.cumsum(chosen, axis=0) - chosen
    slot_ids = jnp.arange(capacity, dtype=jnp.int32)
    selected = (chosen.T[:, None, :] == 1) & (ranking.T[:, None, :] == slot_ids[None, :, None])
    selected_flat = selected.reshape(experts * capacity, tok_dev)
    packed_rows = jnp.dot(
        selected_flat.astype(jnp.bfloat16), tokens, preferred_element_type=jnp.float32
    ).astype(jnp.bfloat16)
    gate_mat = gate_proj[0]
    up_mat = up_proj[0]
    down_mat = down_proj[0]
    packed = jnp.broadcast_to(
        packed_rows.reshape(experts, 1, capacity, features), (experts, wsplit, capacity, features)
    )
    outgoing = packed.reshape(node_count * local_count, capacity, features)
    outputs = expert_rows(
        lax.all_to_all(outgoing, ("node", "local"), split_axis=0, concat_axis=0, tiled=True),
        gate_mat,
        up_mat,
        down_mat,
    )
    returned = lax.all_to_all(outputs, ("node", "local"), split_axis=0, concat_axis=0, tiled=True)
    summed = jnp.sum(
        returned.reshape(experts, wsplit, capacity, features).astype(jnp.float32), axis=1
    )
    summed = summed.reshape(experts * capacity, features)
    slot_rank = jnp.take_along_axis(ranking, expert_ids, axis=1)
    row_index = expert_ids * capacity + slot_rank
    picked = summed[row_index]
    combined = jnp.sum(picked * gate_weights[:, :, None], axis=1)
    return combined.astype(jnp.bfloat16)


def solution(mesh):
    return jax.shard_map(
        on_device,
        mesh=mesh,
        in_specs=(
            P(("parts", "node", "local"), None),
            P(("parts", "node", "local"), None),
            P(("parts", "node", "local"), None),
            P(("node", "local"), None, None),
            P(("node", "local"), None, None),
            P(("node", "local"), None, None),
        ),
        out_specs=P(("parts", "node", "local"), None),
        check_vma=False,
    )
```

profile of v0, /device:TPU:0, one launch (start us, length us, event | category | flops | bytes accessed | tf_op | source)
XLA Modules:
  0.0 237.1 jit_solution(13579295022008865182)
XLA Ops:
  0.0 0.8 convert_reduce_fusion
  0.8 0.1 copy.33
  0.9 0.2 reduce_window_sum.11
  1.1 0.1 eq.52
  1.2 0.2 fusion.13
  1.4 1.1 convolution_convert_fusion
  2.5 90.6 %all_to_all.10 = bf16[16,32,3584]{2,1,0:T(8,128)(2,1)S(1)} all-to-all(bf16[16,32,3584]{2,1,0:T(8,128)(2,1)S(1)} %bitcast.39), channel_id=1, replica_groups=mesh['parts'=2,'node'=4,'local'=4] {'node','local'}, dimensions={0} | all-to-all | bytes 7340032 | tf_op jit(solution)/shard_map/all_to_all | solution.py:45
  93.1 1.8 copy-done.1
  94.9 3.9 %fusion.2 = f32[512,1024]{1,0:T(8,128)S(1)} fusion(bf16[512,3584]{1,0:T(8,128)(2,1)S(1)} %bitcast.41, bf16[1,3584,1024]{2,1,0:T(8,128)(2,1)S(1)} %copy-done.4), kind=kOutput, calls=%fused_computation.4 | convolution fusion | flops 3758096384 | bytes 13107200 | tf_op jit(solution)/shard_map/dot_general | solution.py:13
  98.9 16.0 %fusion.6 = bf16[512,3584]{1,0:T(8,128)(2,1)} fusion(bf16[1,1024,3584]{2,1,0:T(8,128)(2,1)} %param.11, f32[512,1024]{1,0:T(8,128)S(1)} %fusion.2, bf16[512,3584]{1,0:T(8,128)(2,1)} %bitcast.42, bf16[1,3584,1024]{2,1,0:T(8,128)(2,1)} %param.9), kind=kOutput, calls=%fused_computation.9 | convolution fusion | flops 7521173504 | bytes 24117248 | tf_op jit(solution)/shard_map/dot_general | solution.py:15
  114.9 4.8 %all-to-all-start.1 = ((bf16[16,32,3584]{2,1,0:T(8,128)(2,1)}), bf16[16,32,3584]{2,1,0:T(8,128)(2,1)}, u32[]{:S(2)}, u32[]{:S(2)}) async-start(bf16[16,32,3584]{2,1,0:T(8,128)(2,1)} %bitcast.40), calls=%async_computation.1 | async-start | bytes 7340032 | tf_op jit(solution)/shard_map/all_to_all | solution.py:50
  119.7 0.1 copy.36
  119.8 0.2 reshape.50
  120.0 2.9 %gather_fusion.1 = s32[384]{0:T(512)S(1)} fusion(s32[128,16]{1,0:T(8,128)S(1)} %sub.7, s32[384]{0:T(512)S(1)} %reshape.50), kind=kCustom, calls=%fused_computation.1 | custom fusion | bytes 6144 | tf_op jit(solution)/shard_map/jit(take_along_axis)/gather | solution.py:55
  122.9 0.2 reshape.53
  123.1 0.1 copy.37
  123.2 0.1 copy.38
  123.3 0.2 reshape.44
  123.6 0.1 copy.39
  123.7 79.0 %all-to-all-done.1 = bf16[16,32,3584]{2,1,0:T(8,128)(2,1)} async-done(((bf16[16,32,3584]{2,1,0:T(8,128)(2,1)}), bf16[16,32,3584]{2,1,0:T(8,128)(2,1)}, u32[]{:S(2)}, u32[]{:S(2)}) %all-to-all-start.1) | async-done | bytes 3670048 | tf_op jit(solution)/shard_map/all_to_all | solution.py:50
  202.6 6.0 %bitcast_convert_fusion = f32[512,3584]{1,0:T(8,128)} fusion(bf16[16,32,3584]{2,1,0:T(8,128)(2,1)} %all-to-all-done.1), kind=kLoop, calls=%fused_computation.11 | loop fusion | flops 1835008 | bytes 11010048 | tf_op jit(solution)/shard_map/reshape | solution.py:54
  208.6 10.7 %gather_fusion = f32[384,3584]{1,0:T(8,128)} fusion(f32[512,3584]{1,0:T(8,128)} %bitcast_convert_fusion, s32[1024]{0:T(1024)S(1)} %pad_clamp_fusion), kind=kCustom, calls=%fused_computation | custom fusion | bytes 11011584 | tf_op jit(solution)/shard_map/gather | solution.py:57
  219.3 8.5 %reshape.43 = f32[128,3,3584]{2,1,0:T(4,128)} reshape(f32[384,3584]{1,0:T(8,128)} %gather_fusion) | data formatting | bytes 11010048 | tf_op jit(solution)/shard_map/gather | solution.py:57
  227.8 9.3 %multiply_reduce_fusion = bf16[128,3584]{1,0:T(8,128)(2,1)} fusion(f32[128,3,3584]{2,1,0:T(4,128)} %reshape.43, f32[128,3]{1,0:T(8,128)S(1)} %copy.39), kind=kLoop, calls=%fused_computation.8 | loop fusion | flops 2293760 | bytes 6424064 | tf_op jit(solution)/shard_map/reduce_sum | solution.py:58
  (16 shorter events, 0.1 us)
Async XLA Ops:
  0.0 1.4 copy-start
  1.4 93.6 %copy-start.4 = (bf16[1,3584,1024]{2,1,0:T(8,128)(2,1)S(1)}, bf16[1,3584,1024]{2,1,0:T(8,128)(2,1)}, u32[]{:S(2)}) copy-start(bf16[1,3584,1024]{2,1,0:T(8,128)(2,1)} %param.10) | copy-start | bytes 22020100
  93.1 1.8 copy-start.1
  114.9 4.8 %copy-start.2 = (s32[128,3]{0,1:T(4,128)S(1)}, s32[128,3]{0,1:T(4,128)}, u32[]{:S(2)}) copy-start(s32[128,3]{0,1:T(4,128)} %param.7) | copy-start | bytes 4612
  114.9 87.8 %all-to-all-start.1 = ((bf16[16,32,3584]{2,1,0:T(8,128)(2,1)}), bf16[16,32,3584]{2,1,0:T(8,128)(2,1)}, u32[]{:S(2)}, u32[]{:S(2)}) async-start(bf16[16,32,3584]{2,1,0:T(8,128)(2,1)} %bitcast.40), calls=%async_computation.1 | async-start | bytes 7340032 | tf_op jit(solution)/shard_map/all_to_all | solution.py:50
  120.0 3.5 %copy-start.3 = (f32[128,3]{0,1:T(4,128)S(1)}, f32[128,3]{0,1:T(4,128)}, u32[]{:S(2)}) copy-start(f32[128,3]{0,1:T(4,128)} %param.8) | copy-start | bytes 4612
where the time goes:
time: 238 us; the launch traced here: 237 us
  blocking collectives  90.6 us (38%)
  waiting for transfers between devices  79 us (33%)
  local copies, waits for them, and re-layouts  25.2 us (11%)
  matrix products  21 us (9%)
  other arithmetic  16.4 us (7%)
  starting transfers between devices  4.82 us (2%)
    all_to_all x1, blocking collectives, on_device(): lax.all_to_all(outgoing, ('node', 'local'), split_axis=0, concat_axis=0,...  90.6 us
    all_to_all x1, waiting for transfers between devices, on_device(): lax.all_to_all(outputs, ('node', 'local'), split_axis=0, concat_axis=0, t...  79 us
    gather x2, local copies, waits for them, and re-layouts, on_device(): picked = summed[row_index]  19.2 us
    dot_general x1, matrix products, expert_rows(): jnp.dot(hidden, down_mat, preferred_element_type=jnp.float32)  16 us
    reduce_sum x1, other arithmetic, on_device(): combined = jnp.sum(picked * gate_weights[:, :, None], axis=1)  9.26 us
    reshape x1, other arithmetic, on_device(): summed = summed.reshape(experts * capacity, features)  5.96 us
    all_to_all x1, starting transfers between devices, on_device(): lax.all_to_all(outputs, ('node', 'local'), split_axis=0, concat_axis=0, t...  4.82 us
  transfers between devices with their start and end apart: 1, of which 1 were waited for; matrix products, arithmetic and copies ran while one was open for 2% of the time, Pallas kernels for 0%

commit v1 on v0

v1 whole, which is shorter than its diff:
```python
import functools

import jax
import jax.numpy as jnp
from jax import lax
from jax.experimental import pallas as pl
from jax.experimental.pallas import tpu as pltpu
from jax.sharding import PartitionSpec as P

EPG = 4
CHUNKS = 4
VMEM_BUDGET = 60 * 1024 * 1024
MESH = pl.DeviceIdType.MESH


def routing(expert_ids, experts):
    matches = expert_ids[:, :, None] == jnp.arange(experts, dtype=jnp.int32)[None, None, :]
    chosen = jnp.sum(matches.astype(jnp.int32), axis=1)
    ranking = jnp.cumsum(chosen, axis=0) - chosen
    rank = jnp.sum(jnp.where(matches, ranking[:, None, :], 0), axis=2)
    return rank


def split_weight(weight):
    high = weight.astype(jnp.bfloat16)
    low = (weight - high.astype(jnp.float32)).astype(jnp.bfloat16)
    return high, low


def expert_rows(received, gate_mat, up_mat, down_mat):
    features = received.shape[-1]
    flattened = received.reshape(-1, features)
    gate_act = jnp.dot(flattened, gate_mat, preferred_element_type=jnp.float32)
    up_act = jnp.dot(flattened, up_mat, preferred_element_type=jnp.float32)
    hidden = (jax.nn.silu(gate_act) * up_act).astype(jnp.bfloat16)
    output = jnp.dot(hidden, down_mat, preferred_element_type=jnp.float32).astype(jnp.bfloat16)
    return output.reshape(received.shape)


def by_collectives(tokens, codes, gate_weights, gate_proj, up_proj, down_proj, experts, wsplit, capacity):
    tok_dev, features = tokens.shape
    slots = jnp.arange(experts * capacity, dtype=jnp.int32)
    hit = codes[:, :, None] == slots[None, None, :]
    selected = jnp.any(hit, axis=1).astype(jnp.bfloat16).T
    packed = jnp.dot(selected, tokens, preferred_element_type=jnp.float32).astype(jnp.bfloat16)
    packed = jnp.broadcast_to(
        packed.reshape(experts, 1, capacity, features), (experts, wsplit, capacity, features)
    ).reshape(experts * wsplit, capacity, features)
    outputs = expert_rows(
        lax.all_to_all(packed, ("node", "local"), split_axis=0, concat_axis=0, tiled=True),
        gate_proj[0], up_proj[0], down_proj[0],
    )
    returned = lax.all_to_all(outputs, ("node", "local"), split_axis=0, concat_axis=0, tiled=True)
    weight = jnp.sum(jnp.where(hit, gate_weights[:, :, None], 0.0), axis=1)
    weight = jnp.broadcast_to(
        weight.reshape(tok_dev, experts, 1, capacity), (tok_dev, experts, wsplit, capacity)
    ).reshape(tok_dev, -1)
    high, low = split_weight(weight)
    returned = returned.reshape(-1, features)
    combined = jnp.dot(high, returned, preferred_element_type=jnp.float32)
    combined = combined + jnp.dot(low, returned, preferred_element_type=jnp.float32)
    return combined.astype(jnp.bfloat16)


def kernel(
    nodes, planes, wsplit, capacity, topk,
    tok_ref, meta_ref, gate_hbm, up_hbm, down_hbm, out_ref,
    gath, metas, pack, recv, ret, inc, hid, wg, wu, wd,
    w_sem, g_send, g_recv, m_send, m_recv, p_send, p_recv, r_send, r_recv, i_send, i_recv,
):
    n = lax.axis_index("node")
    l = lax.axis_index("local")
    tok, features = tok_ref.shape
    ff = wg.shape[1]
    slots = nodes * capacity
    rows = tok // CHUNKS

    def other_node(d):
        return lax.rem(n + d, nodes)

    def other_plane(d):
        return lax.rem(l + d, planes)

    barrier = pltpu.get_barrier_semaphore()
    for d in range(1, nodes):
        pl.semaphore_signal(barrier, inc=1, device_id={"node": other_node(d)}, device_id_type=MESH)
    for d in range(1, planes):
        pl.semaphore_signal(barrier, inc=1, device_id={"local": other_plane(d)}, device_id_type=MESH)

    loads = [
        pltpu.make_async_copy(gate_hbm.at[0], wg, w_sem.at[0]),
        pltpu.make_async_copy(up_hbm.at[0], wu, w_sem.at[1]),
        pltpu.make_async_copy(down_hbm.at[0], wd, w_sem.at[2]),
    ]
    for load in loads:
        load.start()
    gath[l] = tok_ref[...]
    metas[l] = meta_ref[...]
    pl.semaphore_wait(barrier, nodes - 1 + planes - 1)

    def block_copy(src, way, plane):
        return pltpu.make_async_remote_copy(
            src_ref=gath.at[src], dst_ref=gath.at[src], send_sem=g_send.at[way, src], recv_sem=g_recv.at[src],
            device_id={"local": plane}, device_id_type=MESH,
        )

    def meta_copy(src, plane):
        return pltpu.make_async_remote_copy(
            src_ref=metas.at[src], dst_ref=metas.at[src], send_sem=m_send.at[plane], recv_sem=m_recv.at[src],
            device_id={"local": plane}, device_id_type=MESH,
        )

    def pack_copy(src, to, slot):
        return pltpu.make_async_remote_copy(
            src_ref=pack.at[src, to], dst_ref=recv.at[src, slot], send_sem=p_send.at[src, to], recv_sem=p_recv.at[src, slot],
            device_id={"node": to}, device_id_type=MESH,
        )

    def ret_copy(src, to, slot):
        return pltpu.make_async_remote_copy(
            src_ref=recv.at[src, to], dst_ref=ret.at[src, slot], send_sem=r_send.at[src, to], recv_sem=r_recv.at[src, slot],
            device_id={"node": to}, device_id_type=MESH,
        )

    def inc_copy(src, slot, chunk, plane):
        part = pl.ds(pl.multiple_of(chunk * rows, rows), rows)
        return pltpu.make_async_remote_copy(
            src_ref=inc.at[src, part], dst_ref=inc.at[slot, part], send_sem=i_send.at[src, chunk], recv_sem=i_recv.at[slot, chunk],
            device_id={"local": plane}, device_id_type=MESH,
        )

    for d in range(1, planes):
        meta_copy(l, other_plane(d)).start()

    def forward(src):
        @pl.when((src <= l) & (l < planes - 1))
        def _():
            block_copy(src, 0, l + 1).start()

        @pl.when((src >= l) & (l > 0))
        def _():
            block_copy(src, 1, l - 1).start()

    paired = jnp.minimum(l, planes - 1 - l)

    def source(j):
        near = (j + 1) // 2
        near = jnp.where(j % 2 == 1, l - near, l + near)
        far = j - paired
        far = jnp.where(l > planes - 1 - l, l - far, l + far)
        return jnp.where(j <= 2 * paired, near, far)

    def slot_codes():
        slot = lax.broadcasted_iota(jnp.int32, (slots, tok), 0)
        code = (slot // capacity) * (EPG * capacity) + (l // wsplit) * capacity + slot % capacity
        return code.astype(jnp.float32)

    def stage_pack(src):
        codes = slot_codes()
        selected = jnp.zeros((slots, tok), jnp.float32)
        for k in range(topk):
            selected = jnp.where(codes == metas[src, k : k + 1, :], 1.0, selected)
        selected = selected.astype(jnp.bfloat16)
        width = 512 if features % 512 == 0 else features

        @pl.loop(0, features // width)
        def _(c):
            cols = pl.ds(pl.multiple_of(c * width, width), width)
            part = jnp.dot(selected, gath[src, :, cols], preferred_element_type=jnp.float32)
            pack[src, :, :, cols] = part.astype(jnp.bfloat16).reshape(nodes, capacity, width)

        for d in range(1, nodes):
            pack_copy(src, other_node(d), n).start()
        recv[src, n] = pack[src, n]

    def stage_expert(src):
        for d in range(1, nodes):
            pack_copy(src, other_node(d), other_node(d)).wait_recv()
        width = 256 if ff % 256 == 0 else ff

        @pl.loop(0, ff // width)
        def _(c):
            cols = pl.ds(pl.multiple_of(c * width, width), width)
            x = recv[src].reshape(slots, features)
            gate = jnp.dot(x, wg[:, cols], preferred_element_type=jnp.float32)
            up = jnp.dot(x, wu[:, cols], preferred_element_type=jnp.float32)
            hid[:, cols] = (gate / (1.0 + jnp.exp(-gate)) * up).astype(jnp.bfloat16)

        wide = 512 if features % 512 == 0 else features

        @pl.loop(0, features // wide)
        def _(c):
            cols = pl.ds(pl.multiple_of(c * wide, wide), wide)
            part = jnp.dot(hid[...], wd[:, cols], preferred_element_type=jnp.float32)
            recv[src, :, :, cols] = part.astype(jnp.bfloat16).reshape(nodes, capacity, wide)

        for d in range(1, nodes):
            ret_copy(src, other_node(d), n).start()
        ret[src, n] = recv[src, n]

    def weights_of(src):
        codes = slot_codes()
        weight = jnp.zeros((slots, tok), jnp.float32)
        for k in range(topk):
            weight = jnp.where(codes == metas[src, k : k + 1, :], metas[src, topk + k : topk + k + 1, :], weight)
        return split_weight(weight.T)

    def wait_returned(src):
        for d in range(1, nodes):
            ret_copy(src, other_node(d), other_node(d)).wait_recv()

    def weighted(high, low, src, chunk):
        values = ret[src].reshape(slots, features)
        take = slice(chunk * rows, (chunk + 1) * rows)
        total = jnp.dot(high[take], values, preferred_element_type=jnp.float32)
        return total + jnp.dot(low[take], values, preferred_element_type=jnp.float32)

    def send_partial(src, chunk):
        @pl.when(src < l)
        def _():
            inc_copy(src, src, chunk, l - 1).start()

        @pl.when((src > l) & (src == l + 1))
        def _():
            inc_copy(src, planes, chunk, l + 1).start()

        @pl.when((src > l) & (src != l + 1))
        def _():
            inc_copy(src, src, chunk, l + 1).start()

    def stage_first(src):
        wait_returned(src)
        high, low = weights_of(src)
        for chunk in range(CHUNKS):
            inc[src, chunk * rows : (chunk + 1) * rows, :] = weighted(high, low, src, chunk).astype(jnp.bfloat16)
            send_partial(src, chunk)

    def stage_add(src):
        wait_returned(src)
        high, low = weights_of(src)
        for chunk in range(CHUNKS):
            total = weighted(high, low, src, chunk)
            inc_copy(src, src, chunk, other_plane(1)).wait_recv()
            part = slice(chunk * rows, (chunk + 1) * rows)
            inc[src, part, :] = (total + inc[src, part, :].astype(jnp.float32)).astype(jnp.bfloat16)
            send_partial(src, chunk)

    at_end = (l == 0) | (l == planes - 1)

    def step(j, carry):
        src = source(j)

        @pl.when(j > 0)
        def _():
            block_copy(src, 0, other_plane(1)).wait_recv()
            meta_copy(src, other_plane(1)).wait_recv()

        forward(src)
        stage_pack(src)

        @pl.when(j == 0)
        def _():
            for load in loads:
                load.wait()

        @pl.when((j > 1) & at_end)
        def _():
            stage_first(source(j - 1))

        stage_expert(src)
        return carry

    lax.fori_loop(0, planes, step, 0)

    @pl.when(at_end)
    def _():
        stage_first(source(planes - 1))

    @pl.when(jnp.logical_not(at_end))
    def _():
        def add(i, carry):
            stage_add(source(planes - 1 - i))
            return carry

        lax.fori_loop(0, planes - 1, add, 0)

    wait_returned(l)
    high, low = weights_of(l)
    for chunk in range(CHUNKS):
        part = slice(chunk * rows, (chunk + 1) * rows)

        @pl.when(l < planes - 1)
        def _():
            inc_copy(l, l, chunk, other_plane(1)).wait_recv()

        @pl.when(l > 0)
        def _():
            inc_copy(l, planes, chunk, other_plane(1)).wait_recv()

        right = jnp.where(l < planes - 1, inc[l, part, :].astype(jnp.float32), 0.0)
        left = jnp.where(l > 0, inc[planes, part, :].astype(jnp.float32), 0.0)
        out_ref[part, :] = (weighted(high, low, l, chunk) + right + left).astype(jnp.bfloat16)

    for d in range(1, planes):
        meta_copy(l, other_plane(d)).wait_send()

    def drain(src, carry):
        @pl.when((src <= l) & (l < planes - 1))
        def _():
            block_copy(src, 0, l + 1).wait_send()

        @pl.when((src >= l) & (l > 0))
        def _():
            block_copy(src, 1, l - 1).wait_send()

        for d in range(1, nodes):
            pack_copy(src, other_node(d), n).wait_send()
            ret_copy(src, other_node(d), n).wait_send()

        @pl.when(src != l)
        def _():
            for chunk in range(CHUNKS):
                inc_copy(src, src, chunk, other_plane(1)).wait_send()

        return carry

    lax.fori_loop(0, planes, drain, 0)


def on_device(tokens, expert_ids, gate_weights, gate_proj, up_proj, down_proj):
    tok_dev, features = tokens.shape
    topk = expert_ids.shape[1]
    ff = gate_proj.shape[2]
    nodes = lax.axis_size("node")
    planes = lax.axis_size("local")
    experts = EPG * nodes
    wsplit = planes // EPG
    capacity = 4 * tok_dev * topk // (3 * experts)
    codes = expert_ids * capacity + routing(expert_ids, experts)
    block = nodes * capacity * features * 2
    token_block = tok_dev * features * 2
    needed = planes * 3 * block + (2 * planes + 3) * token_block + 3 * features * ff * 2
    if needed > VMEM_BUDGET - 8 * 1024 * 1024 or planes < 2:
        return by_collectives(
            tokens, codes, gate_weights, gate_proj, up_proj, down_proj, experts, wsplit, capacity
        )
    meta_rows = -(-2 * topk // 8) * 8
    meta = jnp.concatenate(
        [codes.T.astype(jnp.float32), gate_weights.T, jnp.zeros((meta_rows - 2 * topk, tok_dev), jnp.float32)]
    )
    bf16 = jnp.bfloat16
    dma = pltpu.SemaphoreType.DMA
    vmem = pl.BlockSpec(memory_space=pltpu.VMEM)
    anywhere = pl.BlockSpec(memory_space=pl.ANY)
    return pl.pallas_call(
        functools.partial(kernel, nodes, planes, wsplit, capacity, topk),
        out_shape=jax.ShapeDtypeStruct((tok_dev, features), bf16),
        in_specs=[vmem, vmem, anywhere, anywhere, anywhere],
        out_specs=vmem,
        scratch_shapes=[
            pltpu.VMEM((planes, tok_dev, features), bf16),
            pltpu.VMEM((planes, meta_rows, tok_dev), jnp.float32),
            pltpu.VMEM((planes, nodes, capacity, features), bf16),
            pltpu.VMEM((planes, nodes, capacity, features), bf16),
            pltpu.VMEM((planes, nodes, capacity, features), bf16),
            pltpu.VMEM((planes + 1, tok_dev, features), bf16),
            pltpu.VMEM((nodes * capacity, ff), bf16),
            pltpu.VMEM((features, ff), bf16),
            pltpu.VMEM((features, ff), bf16),
            pltpu.VMEM((ff, features), bf16),
            dma((3,)),
            dma((2, planes)),
            dma((planes,)),
            dma((planes,)),
            dma((planes,)),
            dma((planes, nodes)),
            dma((planes, nodes)),
            dma((planes, nodes)),
            dma((planes, nodes)),
            dma((planes, CHUNKS)),
            dma((planes + 1, CHUNKS)),
        ],
        compiler_params=pltpu.CompilerParams(
            collective_id=0, has_side_effects=True, vmem_limit_bytes=VMEM_BUDGET
        ),
    )(tokens, meta, gate_proj, up_proj, down_proj)


def solution(mesh):
    return jax.shard_map(
        on_device,
        mesh=mesh,
        in_specs=(
            P(("parts", "node", "local"), None),
            P(("parts", "node", "local"), None),
            P(("parts", "node", "local"), None),
            P(("node", "local"), None, None),
            P(("node", "local"), None, None),
            P(("node", "local"), None, None),
        ),
        out_specs=P(("parts", "node", "local"), None),
        check_vma=False,
    )
```

time: 238 us -> 171 us (0.72)
  the two profiles are of different devices: /device:TPU:0 before, /device:TPU:13 now
where the time goes in v1:
time: 171 us
  Pallas kernels  165 us (96%)
  other arithmetic  3.62 us (2%)
  local copies, waits for them, and re-layouts  2.39 us (1%)
    pallas_call x1, Pallas kernels, on_device(): pl.pallas_call(functools.partial(kernel, nodes, planes, wsplit, capacity,...  165 us

profile of v1, /device:TPU:13, one launch (start us, length us, event | category | flops | bytes accessed | tf_op | source)
XLA Modules:
  0.0 171.2 jit_solution(9304983265946735788)
XLA Ops:
  0.0 0.1 pad.2.clone
  0.1 0.7 convert_reduce_fusion
  0.8 0.1 copy.8
  0.9 0.2 reduce_window_sum.11
  1.1 0.1 copy.10
  1.1 0.7 select_reduce_fusion
  1.8 0.7 convert_bitcast_fusion
  2.5 1.3 maximum_maximum_fusion.meta_ref
  3.9 165.2 %shard_map.64 = bf16[128,3584]{1,0:T(8,128)(2,1)} custom-call(bf16[128,3584]{1,0:T(8,128)(2,1)} %tok_ref.1, f32[8,128]{1,0:T(8,128)} %maximum_maximum_fusion.meta_ref, bf16[1,3584,1024]{2,1,0:T(8,128)(2,1)} %gate_hbm.1, bf16[1,3584,1024]{2,1,0:T(8,128)(2,1)} %up_hbm.1, bf16[1,1024,3584]{2,1,0:T(8,128)(2,1)} %down_hbm.1), custom_call_target="tpu_custom_call" | custom-call | tf_op jit(solution)/shard_map/pallas_call | solution.py:355
  169.1 2.2 %copy.12 = bf16[128,3584]{1,0:T(8,128)(2,1)} copy(bf16[128,3584]{1,0:T(8,128)(2,1)} %shard_map.64) | data formatting | bytes 1835008
  (2 shorter events, 0.0 us)

commit v2 on v1

v2 whole, which is shorter than its diff:
```python
import functools

import jax
import jax.numpy as jnp
from jax import lax
from jax.experimental import pallas as pl
from jax.experimental.pallas import tpu as pltpu
from jax.sharding import PartitionSpec as P

EPG = 4
CHUNKS = 4
VMEM_BUDGET = 60 * 1024 * 1024
MESH = pl.DeviceIdType.MESH


def routing(expert_ids, experts):
    matches = expert_ids[:, :, None] == jnp.arange(experts, dtype=jnp.int32)[None, None, :]
    chosen = jnp.sum(matches.astype(jnp.int32), axis=1)
    ranking = jnp.cumsum(chosen, axis=0) - chosen
    rank = jnp.sum(jnp.where(matches, ranking[:, None, :], 0), axis=2)
    return rank


def split_weight(weight):
    high = weight.astype(jnp.bfloat16)
    low = (weight - high.astype(jnp.float32)).astype(jnp.bfloat16)
    return high, low


def expert_rows(received, gate_mat, up_mat, down_mat):
    features = received.shape[-1]
    flattened = received.reshape(-1, features)
    gate_act = jnp.dot(flattened, gate_mat, preferred_element_type=jnp.float32)
    up_act = jnp.dot(flattened, up_mat, preferred_element_type=jnp.float32)
    hidden = (jax.nn.silu(gate_act) * up_act).astype(jnp.bfloat16)
    output = jnp.dot(hidden, down_mat, preferred_element_type=jnp.float32).astype(jnp.bfloat16)
    return output.reshape(received.shape)


def by_collectives(tokens, codes, gate_weights, gate_proj, up_proj, down_proj, experts, wsplit, capacity):
    tok_dev, features = tokens.shape
    slots = jnp.arange(experts * capacity, dtype=jnp.int32)
    hit = codes[:, :, None] == slots[None, None, :]
    selected = jnp.any(hit, axis=1).astype(jnp.bfloat16).T
    packed = jnp.dot(selected, tokens, preferred_element_type=jnp.float32).astype(jnp.bfloat16)
    packed = jnp.broadcast_to(
        packed.reshape(experts, 1, capacity, features), (experts, wsplit, capacity, features)
    ).reshape(experts * wsplit, capacity, features)
    outputs = expert_rows(
        lax.all_to_all(packed, ("node", "local"), split_axis=0, concat_axis=0, tiled=True),
        gate_proj[0], up_proj[0], down_proj[0],
    )
    returned = lax.all_to_all(outputs, ("node", "local"), split_axis=0, concat_axis=0, tiled=True)
    weight = jnp.sum(jnp.where(hit, gate_weights[:, :, None], 0.0), axis=1)
    weight = jnp.broadcast_to(
        weight.reshape(tok_dev, experts, 1, capacity), (tok_dev, experts, wsplit, capacity)
    ).reshape(tok_dev, -1)
    high, low = split_weight(weight)
    returned = returned.reshape(-1, features)
    combined = jnp.dot(high, returned, preferred_element_type=jnp.float32)
    combined = combined + jnp.dot(low, returned, preferred_element_type=jnp.float32)
    return combined.astype(jnp.bfloat16)


def kernel(
    nodes, planes, wsplit, capacity, topk,
    tok_ref, meta_ref, gate_hbm, up_hbm, down_hbm, out_ref,
    gath, metas, sel, wts, pack, recv, ret, inc, gate_acc, up_acc, hid, wg, wu, wd,
    w_sem, g_send, g_recv, m_send, m_recv, p_send, p_recv, r_send, r_recv, i_send, i_recv,
):
    n = lax.axis_index("node")
    l = lax.axis_index("local")
    tok, features = tok_ref.shape
    slots = nodes * capacity
    width = features // CHUNKS
    f32, bf16 = jnp.float32, jnp.bfloat16

    def other_node(d):
        return lax.rem(n + d, nodes)

    def other_plane(d):
        return lax.rem(l + d, planes)

    def columns(c):
        return pl.ds(pl.multiple_of(c * width, width), width)

    barrier = pltpu.get_barrier_semaphore()
    for d in range(1, nodes):
        pl.semaphore_signal(barrier, inc=1, device_id={"node": other_node(d)}, device_id_type=MESH)
    for d in range(1, planes):
        pl.semaphore_signal(barrier, inc=1, device_id={"local": other_plane(d)}, device_id_type=MESH)

    metas[l] = meta_ref[...]
    for c in range(CHUNKS):
        gath[l, c] = tok_ref[:, c * width : (c + 1) * width]
    loads = [
        pltpu.make_async_copy(gate_hbm.at[0], wg, w_sem.at[0]),
        pltpu.make_async_copy(up_hbm.at[0], wu, w_sem.at[1]),
        pltpu.make_async_copy(down_hbm.at[0], wd, w_sem.at[2]),
    ]
    for load in loads:
        load.start()
    pl.semaphore_wait(barrier, nodes - 1 + planes - 1)

    def block_copy(src, c, way, plane):
        return pltpu.make_async_remote_copy(
            src_ref=gath.at[src, c], dst_ref=gath.at[src, c],
            send_sem=g_send.at[way, src, c], recv_sem=g_recv.at[src, c],
            device_id={"local": plane}, device_id_type=MESH,
        )

    def meta_copy(src, plane):
        return pltpu.make_async_remote_copy(
            src_ref=metas.at[src], dst_ref=metas.at[src], send_sem=m_send.at[plane], recv_sem=m_recv.at[src],
            device_id={"local": plane}, device_id_type=MESH,
        )

    def pack_copy(src, c, to, slot):
        return pltpu.make_async_remote_copy(
            src_ref=pack.at[src, c, to], dst_ref=recv.at[src, c, slot],
            send_sem=p_send.at[src, c, to], recv_sem=p_recv.at[src, c, slot],
            device_id={"node": to}, device_id_type=MESH,
        )

    def ret_copy(src, c, to, slot):
        return pltpu.make_async_remote_copy(
            src_ref=recv.at[src, c, to], dst_ref=ret.at[src, c, slot],
            send_sem=r_send.at[src, c, to], recv_sem=r_recv.at[src, c, slot],
            device_id={"node": to}, device_id_type=MESH,
        )

    def inc_copy(src, c, slot, plane):
        return pltpu.make_async_remote_copy(
            src_ref=inc.at[src, c], dst_ref=inc.at[slot, c],
            send_sem=i_send.at[src, c], recv_sem=i_recv.at[slot, c],
            device_id={"local": plane}, device_id_type=MESH,
        )

    def forward(src, c):
        @pl.when((src <= l) & (l < planes - 1))
        def _():
            block_copy(src, c, 0, l + 1).start()

        @pl.when((src >= l) & (l > 0))
        def _():
            block_copy(src, c, 1, l - 1).start()

    for d in range(1, planes):
        meta_copy(l, other_plane(d)).start()

    @pl.loop(0, CHUNKS)
    def _(c):
        forward(l, c)

    paired = jnp.minimum(l, planes - 1 - l)

    def source(j):
        near = (j + 1) // 2
        near = jnp.where(j % 2 == 1, l - near, l + near)
        far = j - paired
        far = jnp.where(l > planes - 1 - l, l - far, l + far)
        return jnp.where(j <= 2 * paired, near, far)

    def route(src):
        slot = lax.broadcasted_iota(jnp.int32, (slots, tok), 0)
        code = (slot // capacity) * (EPG * capacity) + (l // wsplit) * capacity + slot % capacity
        code = code.astype(f32)
        weight = jnp.zeros((slots, tok), f32)
        selected = jnp.zeros((slots, tok), f32)
        for k in range(topk):
            hit = code == metas[src, k : k + 1, :]
            selected = jnp.where(hit, 1.0, selected)
            weight = jnp.where(hit, metas[src, topk + k : topk + k + 1, :], weight)
        sel[src] = selected.astype(bf16)
        high, low = split_weight(weight.T)
        wts[src, 0] = high
        wts[src, 1] = low

    def stage_pack(src, c):
        part = jnp.dot(sel[src], gath[src, c], preferred_element_type=f32)
        pack[src, c] = part.astype(bf16).reshape(nodes, capacity, width)
        for d in range(1, nodes):
            pack_copy(src, c, other_node(d), n).start()
        recv[src, c, n] = pack[src, c, n]

    def stage_up(src, c):
        for d in range(1, nodes):
            pack_copy(src, c, other_node(d), other_node(d)).wait_recv()
        x = recv[src, c].reshape(slots, width)
        gate_acc[...] += jnp.dot(x, wg[columns(c), :], preferred_element_type=f32)
        up_acc[...] += jnp.dot(x, wu[columns(c), :], preferred_element_type=f32)

    def stage_down(src):
        gate = gate_acc[...]
        hid[...] = (gate / (1.0 + jnp.exp(-gate)) * up_acc[...]).astype(bf16)

        @pl.loop(0, CHUNKS)
        def _(c):
            part = jnp.dot(hid[...], wd[:, columns(c)], preferred_element_type=f32)
            recv[src, c] = part.astype(bf16).reshape(nodes, capacity, width)
            for d in range(1, nodes):
                ret_copy(src, c, other_node(d), n).start()
            ret[src, c, n] = recv[src, c, n]

    def weighted(src, c):
        for d in range(1, nodes):
            ret_copy(src, c, other_node(d), other_node(d)).wait_recv()
        both = jnp.dot(
            wts[src].reshape(2 * tok, slots), ret[src, c].reshape(slots, width), preferred_element_type=f32
        )
        return both[:tok] + both[tok:]

    def send_partial(src, c):
        @pl.when(src < l)
        def _():
            inc_copy(src, c, src, l - 1).start()

        @pl.when(src == l + 1)
        def _():
            inc_copy(src, c, planes, l + 1).start()

        @pl.when(src > l + 1)
        def _():
            inc_copy(src, c, src, l + 1).start()

    def stage_first(src, c):
        inc[src, c] = weighted(src, c).astype(bf16)
        send_partial(src, c)

    def stage_add(src, c):
        total = weighted(src, c)
        inc_copy(src, c, src, other_plane(1)).wait_recv()
        inc[src, c] = (total + inc[src, c].astype(f32)).astype(bf16)
        send_partial(src, c)

    at_end = (l == 0) | (l == planes - 1)

    def step(j, carry):
        src = source(j)

        @pl.when(j > 0)
        def _():
            meta_copy(src, other_plane(1)).wait_recv()

        route(src)
        gate_acc[...] = jnp.zeros_like(gate_acc)
        up_acc[...] = jnp.zeros_like(up_acc)

        @pl.loop(0, CHUNKS)
        def _(c):
            @pl.when(j > 0)
            def _():
                block_copy(src, c, 0, other_plane(1)).wait_recv()
                forward(src, c)

            stage_pack(src, c)

            @pl.when((j > 1) & at_end)
            def _():
                stage_first(source(j - 1), c)

            @pl.when((j == 0) & (c == 1))
            def _():
                loads[0].wait()
                loads[1].wait()

            @pl.when(c > 0)
            def _():
                stage_up(src, c - 1)

        stage_up(src, CHUNKS - 1)

        @pl.when(j == 0)
        def _():
            loads[2].wait()

        stage_down(src)
        return carry

    lax.fori_loop(0, planes, step, 0)

    @pl.when(at_end)
    def _():
        @pl.loop(0, CHUNKS)
        def _(c):
            stage_first(source(planes - 1), c)

    nearer_right = l > planes - 1 - l
    toward = jnp.where(nearer_right, 1, -1)
    count = jnp.maximum(l, planes - 1 - l)

    @pl.when(jnp.logical_not(at_end))
    def _():
        def add(i, carry):
            late = i - (count - (planes - 1 - count))

            @pl.loop(0, CHUNKS)
            def _(c):
                stage_add(l - toward * (i + 1), c)

                @pl.when(late >= 0)
                def _():
                    stage_add(l + toward * (late + 1), c)

            return carry

        lax.fori_loop(0, count, add, 0)

    @pl.loop(0, CHUNKS)
    def _(c):
        total = weighted(l, c)

        @pl.when(l < planes - 1)
        def _():
            inc_copy(l, c, l, other_plane(1)).wait_recv()

        @pl.when(l > 0)
        def _():
            inc_copy(l, c, planes, other_plane(1)).wait_recv()

        right = jnp.where(l < planes - 1, inc[l, c].astype(f32), 0.0)
        left = jnp.where(l > 0, inc[planes, c].astype(f32), 0.0)
        out_ref[:, columns(c)] = (total + right + left).astype(bf16)

    for d in range(1, planes):
        meta_copy(l, other_plane(d)).wait_send()

    def drain(src, carry):
        @pl.loop(0, CHUNKS)
        def _(c):
            @pl.when((src <= l) & (l < planes - 1))
            def _():
                block_copy(src, c, 0, l + 1).wait_send()

            @pl.when((src >= l) & (l > 0))
            def _():
                block_copy(src, c, 1, l - 1).wait_send()

            for d in range(1, nodes):
                pack_copy(src, c, other_node(d), n).wait_send()
                ret_copy(src, c, other_node(d), n).wait_send()

            @pl.when(src != l)
            def _():
                inc_copy(src, c, src, other_plane(1)).wait_send()

        return carry

    lax.fori_loop(0, planes, drain, 0)


def on_device(tokens, expert_ids, gate_weights, gate_proj, up_proj, down_proj):
    tok_dev, features = tokens.shape
    topk = expert_ids.shape[1]
    ff = gate_proj.shape[2]
    nodes = lax.axis_size("node")
    planes = lax.axis_size("local")
    experts = EPG * nodes
    wsplit = planes // EPG
    capacity = 4 * tok_dev * topk // (3 * experts)
    codes = expert_ids * capacity + routing(expert_ids, experts)
    block = nodes * capacity * features * 2
    token_block = tok_dev * features * 2
    needed = planes * 3 * block + (2 * planes + 3) * token_block + 3 * features * ff * 2
    if needed > VMEM_BUDGET - 8 * 1024 * 1024 or planes != EPG or features % CHUNKS:
        return by_collectives(
            tokens, codes, gate_weights, gate_proj, up_proj, down_proj, experts, wsplit, capacity
        )
    meta_rows = -(-2 * topk // 8) * 8
    meta = jnp.concatenate(
        [codes.T.astype(jnp.float32), gate_weights.T, jnp.zeros((meta_rows - 2 * topk, tok_dev), jnp.float32)]
    )
    width = features // CHUNKS
    bf16 = jnp.bfloat16
    dma = pltpu.SemaphoreType.DMA
    vmem = pl.BlockSpec(memory_space=pltpu.VMEM)
    anywhere = pl.BlockSpec(memory_space=pl.ANY)
    return pl.pallas_call(
        functools.partial(kernel, nodes, planes, wsplit, capacity, topk),
        out_shape=jax.ShapeDtypeStruct((tok_dev, features), bf16),
        in_specs=[vmem, vmem, anywhere, anywhere, anywhere],
        out_specs=vmem,
        scratch_shapes=[
            pltpu.VMEM((planes, CHUNKS, tok_dev, width), bf16),
            pltpu.VMEM((planes, meta_rows, tok_dev), jnp.float32),
            pltpu.VMEM((planes, nodes * capacity, tok_dev), bf16),
            pltpu.VMEM((planes, 2, tok_dev, nodes * capacity), bf16),
            pltpu.VMEM((planes, CHUNKS, nodes, capacity, width), bf16),
            pltpu.VMEM((planes, CHUNKS, nodes, capacity, width), bf16),
            pltpu.VMEM((planes, CHUNKS, nodes, capacity, width), bf16),
            pltpu.VMEM((planes + 1, CHUNKS, tok_dev, width), bf16),
            pltpu.VMEM((nodes * capacity, ff), jnp.float32),
            pltpu.VMEM((nodes * capacity, ff), jnp.float32),
            pltpu.VMEM((nodes * capacity, ff), bf16),
            pltpu.VMEM((features, ff), bf16),
            pltpu.VMEM((features, ff), bf16),
            pltpu.VMEM((ff, features), bf16),
            dma((3,)),
            dma((2, planes, CHUNKS)),
            dma((planes, CHUNKS)),
            dma((planes,)),
            dma((planes,)),
            dma((planes, CHUNKS, nodes)),
            dma((planes, CHUNKS, nodes)),
            dma((planes, CHUNKS, nodes)),
            dma((planes, CHUNKS, nodes)),
            dma((planes, CHUNKS)),
            dma((planes + 1, CHUNKS)),
        ],
        compiler_params=pltpu.CompilerParams(
            collective_id=0, has_side_effects=True, vmem_limit_bytes=VMEM_BUDGET
        ),
    )(tokens, meta, gate_proj, up_proj, down_proj)


def solution(mesh):
    return jax.shard_map(
        on_device,
        mesh=mesh,
        in_specs=(
            P(("parts", "node", "local"), None),
            P(("parts", "node", "local"), None),
            P(("parts", "node", "local"), None),
            P(("node", "local"), None, None),
            P(("node", "local"), None, None),
            P(("node", "local"), None, None),
        ),
        out_specs=P(("parts", "node", "local"), None),
        check_vma=False,
    )
```

time: 171 us -> 153 us (0.89)
  the two profiles are of different devices: /device:TPU:13 before, /device:TPU:0 now
where the time goes in v2:
time: 153 us
  Pallas kernels  147 us (96%)
  other arithmetic  3.62 us (2%)
  local copies, waits for them, and re-layouts  2.39 us (2%)
    pallas_call x1, Pallas kernels, on_device(): pl.pallas_call(functools.partial(kernel, nodes, planes, wsplit, capacity,...  147 us

profile of v2, /device:TPU:0, one launch (start us, length us, event | category | flops | bytes accessed | tf_op | source)
XLA Modules:
  0.0 153.1 jit_solution(17208232890183165386)
XLA Ops:
  0.0 0.1 pad.2.clone
  0.1 0.7 convert_reduce_fusion
  0.8 0.1 copy.8
  0.9 0.2 reduce_window_sum.11
  1.1 0.1 copy.10
  1.1 0.7 select_reduce_fusion
  1.8 0.7 convert_bitcast_fusion
  2.5 1.3 maximum_maximum_fusion.meta_ref
  3.9 147.1 %shard_map.64 = bf16[128,3584]{1,0:T(8,128)(2,1)} custom-call(bf16[128,3584]{1,0:T(8,128)(2,1)} %tok_ref.1, f32[8,128]{1,0:T(8,128)} %maximum_maximum_fusion.meta_ref, bf16[1,3584,1024]{2,1,0:T(8,128)(2,1)} %gate_hbm.1, bf16[1,3584,1024]{2,1,0:T(8,128)(2,1)} %up_hbm.1, bf16[1,1024,3584]{2,1,0:T(8,128)(2,1)} %down_hbm.1), custom_call_target="tpu_custom_call" | custom-call | tf_op jit(solution)/shard_map/pallas_call | solution.py:378
  151.0 2.2 %copy.12 = bf16[128,3584]{1,0:T(8,128)(2,1)} copy(bf16[128,3584]{1,0:T(8,128)(2,1)} %shard_map.64) | data formatting | bytes 1835008
  (2 shorter events, 0.0 us)

commit v3 on v2

--- a/solution.py
+++ b/solution.py
@@ -235,40 +235,84 @@
 
     at_end = (l == 0) | (l == planes - 1)
 
+    def stage_route(j):
+        src = source(j)
+
+        @pl.when(j > 0)
+        def _():
+            meta_copy(src, other_plane(1)).wait_recv()
+
+        route(src)
+
+    def stage_arrive(j, c):
+        src = source(j)
+
+        @pl.when(j > 0)
+        def _():
+            block_copy(src, c, 0, other_plane(1)).wait_recv()
+            forward(src, c)
+
+        stage_pack(src, c)
+
+    def wait_first_weights(j, c):
+        @pl.when((j == 0) & (c == 0))
+        def _():
+            loads[0].wait()
+            loads[1].wait()
+
+    middle = jnp.logical_not(at_end)
+
+    @pl.when(middle)
+    def _():
+        stage_route(0)
+
+        @pl.loop(0, CHUNKS)
+        def _(c):
+            stage_arrive(0, c)
+
     def step(j, carry):
         src = source(j)
-
-        @pl.when(j > 0)
-        def _():
-            meta_copy(src, other_plane(1)).wait_recv()
-
-        route(src)
+        even = j % 2 == 0
+        next_one = middle & (j + 1 < planes) & (even | (j + 1 > 2 * paired))
+        next_two = middle & even & (j + 2 <= 2 * paired)
+
+        @pl.when(next_one)
+        def _():
+            stage_route(j + 1)
+
+        @pl.when(next_two)
+        def _():
+            stage_route(j + 2)
+
+        @pl.when(at_end)
+        def _():
+            stage_route(j)
+
         gate_acc[...] = jnp.zeros_like(gate_acc)
         up_acc[...] = jnp.zeros_like(up_acc)
 
-        @pl.loop(0, CHUNKS)
+        @pl.loop(0, CHUNKS + 1)
         def _(c):
-            @pl.when(j > 0)
-            def _():
-                block_copy(src, c, 0, other_plane(1)).wait_recv()
-                forward(src, c)
-
-            stage_pack(src, c)
-
-            @pl.when((j > 1) & at_end)
-            def _():
-                stage_first(source(j - 1), c)
-
-            @pl.when((j == 0) & (c == 1))
-            def _():
-                loads[0].wait()
-                loads[1].wait()
+            @pl.when(at_end & (c < CHUNKS))
+            def _():
+                stage_arrive(j, c)
+
+                @pl.when(j > 1)
+                def _():
+                    stage_first(source(j - 1), c)
+
+            @pl.when(next_one & (c < CHUNKS))
+            def _():
+                stage_arrive(j + 1, c)
+
+            @pl.when(next_two & (c < CHUNKS))
+            def _():
+                stage_arrive(j + 2, c)
 
             @pl.when(c > 0)
             def _():
+                wait_first_weights(j, c - 1)
                 stage_up(src, c - 1)
-
-        stage_up(src, CHUNKS - 1)
 
         @pl.when(j == 0)
         def _():
@@ -289,7 +333,7 @@
     toward = jnp.where(nearer_right, 1, -1)
     count = jnp.maximum(l, planes - 1 - l)
 
-    @pl.when(jnp.logical_not(at_end))
+    @pl.when(middle)
     def _():
         def add(i, carry):
             late = i - (count - (planes - 1 - count))

time: 153 us -> 145 us (0.948)
  Pallas kernels: 147 us -> 139 us
    pallas_call x1, Pallas kernels: 147 us -> 139 us  [on_device(): pl.pallas_call(functools.partial(kernel, nodes, planes, wsplit, capacity,...]
where the time goes in v3:
time: 145 us
  Pallas kernels  139 us (96%)
  other arithmetic  3.62 us (2%)
  local copies, waits for them, and re-layouts  2.39 us (2%)
    pallas_call x1, Pallas kernels, on_device(): pl.pallas_call(functools.partial(kernel, nodes, planes, wsplit, capacity,...  139 us

profile of v3, /device:TPU:0, one launch (start us, length us, event | category | flops | bytes accessed | tf_op | source)
XLA Modules:
  0.0 144.7 jit_solution(9764741666674300427)
XLA Ops:
  0.0 0.1 pad.2.clone
  0.1 0.7 convert_reduce_fusion
  0.8 0.1 copy.8
  0.9 0.2 reduce_window_sum.11
  1.1 0.1 copy.10
  1.1 0.7 select_reduce_fusion
  1.8 0.7 convert_bitcast_fusion
  2.5 1.3 maximum_maximum_fusion.meta_ref
  3.9 138.7 %shard_map.64 = bf16[128,3584]{1,0:T(8,128)(2,1)} custom-call(bf16[128,3584]{1,0:T(8,128)(2,1)} %tok_ref.1, f32[8,128]{1,0:T(8,128)} %maximum_maximum_fusion.meta_ref, bf16[1,3584,1024]{2,1,0:T(8,128)(2,1)} %gate_hbm.1, bf16[1,3584,1024]{2,1,0:T(8,128)(2,1)} %up_hbm.1, bf16[1,1024,3584]{2,1,0:T(8,128)(2,1)} %down_hbm.1), custom_call_target="tpu_custom_call" | custom-call | tf_op jit(solution)/shard_map/pallas_call | solution.py:422
  142.6 2.2 %copy.12 = bf16[128,3584]{1,0:T(8,128)(2,1)} copy(bf16[128,3584]{1,0:T(8,128)(2,1)} %shard_map.64) | data formatting | bytes 1835008
  (2 shorter events, 0.0 us)

commit v4 on v3

--- a/solution.py
+++ b/solution.py
@@ -8,7 +8,7 @@
 from jax.sharding import PartitionSpec as P
 
 EPG = 4
-CHUNKS = 4
+CHUNKS = 7
 VMEM_BUDGET = 60 * 1024 * 1024
 MESH = pl.DeviceIdType.MESH
 
@@ -90,7 +90,6 @@
     for d in range(1, planes):
         pl.semaphore_signal(barrier, inc=1, device_id={"local": other_plane(d)}, device_id_type=MESH)
 
-    metas[l] = meta_ref[...]
     for c in range(CHUNKS):
         gath[l, c] = tok_ref[:, c * width : (c + 1) * width]
     loads = [
@@ -145,12 +144,24 @@
         def _():
             block_copy(src, c, 1, l - 1).start()
 
-    for d in range(1, planes):
-        meta_copy(l, other_plane(d)).start()
-
     @pl.loop(0, CHUNKS)
     def _(c):
         forward(l, c)
+
+    experts = EPG * nodes
+    row = lax.broadcasted_iota(jnp.int32, (experts, tok), 0).astype(f32)
+    chosen = jnp.zeros((experts, tok), f32)
+    for k in range(topk):
+        chosen = jnp.where(row == meta_ref[k : k + 1, :], 1.0, chosen)
+    earlier = lax.broadcasted_iota(jnp.int32, (tok, tok), 0) < lax.broadcasted_iota(jnp.int32, (tok, tok), 1)
+    ranks = jnp.dot(chosen.astype(bf16), jnp.where(earlier, 1.0, 0.0).astype(bf16), preferred_element_type=f32)
+    code_of = row * capacity + ranks
+    metas[l] = meta_ref[...]
+    for k in range(topk):
+        picked = jnp.where(row == meta_ref[k : k + 1, :], code_of, 0.0)
+        metas[l, k : k + 1, :] = jnp.sum(picked, axis=0, keepdims=True)
+    for d in range(1, planes):
+        meta_copy(l, other_plane(d)).start()
 
     paired = jnp.minimum(l, planes - 1 - l)
 
@@ -297,10 +308,6 @@
             def _():
                 stage_arrive(j, c)
 
-                @pl.when(j > 1)
-                def _():
-                    stage_first(source(j - 1), c)
-
             @pl.when(next_one & (c < CHUNKS))
             def _():
                 stage_arrive(j + 1, c)
@@ -313,6 +320,10 @@
             def _():
                 wait_first_weights(j, c - 1)
                 stage_up(src, c - 1)
+
+            @pl.when(at_end & (c < CHUNKS) & (j > 1))
+            def _():
+                stage_first(source(j - 1), c)
 
         @pl.when(j == 0)
         def _():
@@ -402,17 +413,17 @@
     experts = EPG * nodes
     wsplit = planes // EPG
     capacity = 4 * tok_dev * topk // (3 * experts)
-    codes = expert_ids * capacity + routing(expert_ids, experts)
     block = nodes * capacity * features * 2
     token_block = tok_dev * features * 2
     needed = planes * 3 * block + (2 * planes + 3) * token_block + 3 * features * ff * 2
     if needed > VMEM_BUDGET - 8 * 1024 * 1024 or planes != EPG or features % CHUNKS:
+        codes = expert_ids * capacity + routing(expert_ids, experts)
         return by_collectives(
             tokens, codes, gate_weights, gate_proj, up_proj, down_proj, experts, wsplit, capacity
         )
     meta_rows = -(-2 * topk // 8) * 8
     meta = jnp.concatenate(
-        [codes.T.astype(jnp.float32), gate_weights.T, jnp.zeros((meta_rows - 2 * topk, tok_dev), jnp.float32)]
+        [expert_ids.T.astype(jnp.float32), gate_weights.T, jnp.zeros((meta_rows - 2 * topk, tok_dev), jnp.float32)]
     )
     width = features // CHUNKS
     bf16 = jnp.bfloat16

time: 145 us -> 159 us (1.097)
  Pallas kernels: 139 us -> 154 us
  other arithmetic: 3.62 us -> 2.03 us
    pallas_call x1, Pallas kernels: 139 us -> 154 us  [on_device(): pl.pallas_call(functools.partial(kernel, nodes, planes, wsplit, capacity,...]
where the time goes in v4:
time: 159 us
  Pallas kernels  154 us (97%)
  local copies, waits for them, and re-layouts  2.24 us (1%)
  other arithmetic  2.03 us (1%)
    pallas_call x1, Pallas kernels, on_device(): pl.pallas_call(functools.partial(kernel, nodes, planes, wsplit, capacity,...  154 us

profile of v4, /device:TPU:0, one launch (start us, length us, event | category | flops | bytes accessed | tf_op | source)
XLA Modules:
  0.0 158.6 jit_solution(3082775767264658049)
XLA Ops:
  0.0 0.1 pad.2.clone
  0.1 0.7 convert_bitcast_fusion
  0.8 1.3 maximum_maximum_fusion.meta_ref
  2.1 154.4 %shard_map.64 = bf16[128,3584]{1,0:T(8,128)(2,1)} custom-call(bf16[128,3584]{1,0:T(8,128)(2,1)} %tok_ref.1, f32[8,128]{1,0:T(8,128)} %maximum_maximum_fusion.meta_ref, bf16[1,3584,1024]{2,1,0:T(8,128)(2,1)} %gate_hbm.1, bf16[1,3584,1024]{2,1,0:T(8,128)(2,1)} %up_hbm.1, bf16[1,1024,3584]{2,1,0:T(8,128)(2,1)} %down_hbm.1), custom_call_target="tpu_custom_call" | custom-call | tf_op jit(solution)/shard_map/pallas_call | solution.py:433
  156.5 2.2 %copy.8 = bf16[128,3584]{1,0:T(8,128)(2,1)} copy(bf16[128,3584]{1,0:T(8,128)(2,1)} %shard_map.64) | data formatting | bytes 1835008
  (1 shorter events, 0.0 us)
